TPU v7x, 32 devices: a whole 2x2x4 slice. The times are simulated.
32 devices in a mesh: section: 2 (over x), ctx: 16 (over z, y, core).
Axes of the slice: x: 2, y: 2, z: 4, core: 2. Of those that a mesh axis runs over, the one named last changes fastest.
Arguments:
- earlier_span: bfloat16 [2, 2048, 4096], P('section', 'ctx'), may hold values from -6 to 6
- span_inputs: bfloat16 [2, 2048, 4096], P('section', 'ctx'), may hold values from -24 to 24
- next_inputs: bfloat16 [2048, 4096], P('ctx'), may hold values from -24 to 24
- block_list: int32 [16, 4], replicated, may hold values from -1 to 31, as said below
- q_gain: float32 [2, 4096], P('section'), may hold values from 0.5 to 8
- k_gain: float32 [2, 4096], P('section'), may hold values from -8 to 8
- out_gain: float32 [2, 4096], P('section'), may hold values from 0.5 to 2
Outputs:
- second_out: bfloat16 [2, 2048, 4096], P('section', 'ctx')
Inputs may be any that keep to these rules, and one draw needn't show every extreme that they name: `block_list`: row i names key block 16 + i, then 16 + i - 1, then 1 increasing blocks r from 0 to 13, the same in every row, then the blocks 16 + r in the same order, each replaced by -1 unless it is at least 2 blocks before 16 + i. The last row has no -1.
All inputs are finite; a program needn't handle non-finite values.
Results may differ from a plain program's by a relative error of at most 0.0055.
The roundings to bfloat16 on the way count: a program that leaves them out, or rounds other values in their place, can miss the bound.
Values may be sent and summed in bfloat16 or wider, within the bound.
A program may use at most 64 MiB of HBM per device.

v0:
```python
import jax
import jax.numpy as jnp
from jax import lax
from jax.sharding import PartitionSpec as P

HEADS = 32
HD = 128
BLOCK = 128
LOCAL = 2
NR = 1
WIDTH = 4096
NSEL = 4


def from_behind(value, axis, steps):
    count = lax.axis_size(axis)
    pairs = [(source, (source + steps) % count) for source in range(count)]
    return lax.ppermute(value, axis, pairs)


def broadcast(value, axis, source):
    kept = jnp.where(lax.axis_index(axis) == source, value, 0).astype(value.dtype)
    return lax.psum(kept, axis)


def passed_along(value, axis, steps):
    count = lax.axis_size(axis)
    initial, last = (max(0, -steps), min(count, count - steps))
    return lax.ppermute(value, axis, [(source, source + steps) for source in range(initial, last)])


def normalize(rows):
    widened = rows.astype(jnp.float32).reshape(rows.shape[0], HEADS, HD)
    return widened * lax.rsqrt(jnp.mean(widened * widened, axis=-1, keepdims=True) + 1e-06)


def attend_block(query_rows, key_rows, entries, global_block, gain_query, gain_key, gain_out):
    key_flat = key_rows.reshape(NSEL * BLOCK, WIDTH)
    queries = (normalize(query_rows) * gain_query.reshape(HEADS, HD) * HD ** (-0.5)).astype(
        jnp.bfloat16
    )
    keys = (normalize(key_flat) * gain_key.reshape(HEADS, HD)).astype(jnp.bfloat16)
    values = key_flat.reshape(NSEL * BLOCK, HEADS, HD)
    key_entry = jnp.repeat(entries, BLOCK)
    key_pos = jnp.arange(NSEL * BLOCK, dtype=jnp.int32) % BLOCK
    query_pos = jnp.arange(BLOCK, dtype=jnp.int32)
    allowed = (key_entry >= 0)[None, :] & (
        (key_entry != global_block)[None, :] | (key_pos[None, :] <= query_pos[:, None])
    )
    scores = jnp.einsum("qhd,khd->hqk", queries, keys, preferred_element_type=jnp.float32)
    scores = jnp.where(allowed[None], scores, -jnp.inf)
    maxima = jnp.max(scores, axis=-1, keepdims=True)
    raw = jnp.exp(scores - maxima)
    totals = jnp.sum(raw, axis=-1)
    weights = raw.astype(jnp.bfloat16)
    context = jnp.einsum("hqk,khd->qhd", weights, values, preferred_element_type=jnp.float32)
    contexts = (context / jnp.transpose(totals)[:, :, None]).reshape(BLOCK, WIDTH)
    return (query_rows.astype(jnp.float32) + gain_out * contexts).astype(jnp.bfloat16)


def local(earlier_span, span_inputs, next_inputs, block_list, q_gain, k_gain, out_gain):
    group_size = lax.axis_size("ctx")
    position = lax.axis_index("ctx")
    section_pos = lax.axis_index("section")
    query_entries = lax.dynamic_index_in_dim(block_list, position, 0, keepdims=False)
    full_entries = block_list[group_size - 1]
    global_block = group_size + position
    gain_query = q_gain[0]
    gain_key = k_gain[0]
    gain_out = out_gain[0]

    def previous(earlier_rows, current_rows):
        payload = jnp.where(position == group_size - 1, earlier_rows, current_rows)
        return from_behind(payload, "ctx", 1)

    def strided(earlier_rows, current_rows, block_entry):
        payload = jnp.where(block_entry < group_size, earlier_rows, current_rows)
        return broadcast(payload, "ctx", block_entry % group_size)

    first_earlier = earlier_span[0]
    first_current = span_inputs[0]
    fetched_one = [
        strided(first_earlier, first_current, full_entries[LOCAL + slot]) for slot in range(2 * NR)
    ]
    key_one = jnp.stack([first_current, previous(first_earlier, first_current)] + fetched_one)
    first_result = attend_block(
        first_current, key_one, query_entries, global_block, gain_query, gain_key, gain_out
    )
    received = passed_along(first_result, "section", 1)
    second_current = jnp.where(section_pos == 0, next_inputs, received)
    fetched_two = [
        strided(first_current, second_current, full_entries[LOCAL + slot]) for slot in range(2 * NR)
    ]
    key_two = jnp.stack([second_current, previous(first_current, second_current)] + fetched_two)
    second_result = attend_block(
        second_current, key_two, query_entries, global_block, gain_query, gain_key, gain_out
    )
    return second_result[None]


def solution(mesh):
    in_specs = (
        P("section", "ctx", None),
        P("section", "ctx", None),
        P("ctx", None),
        P(),
        P("section", None),
        P("section", None),
        P("section", None),
    )
    out_specs = P("section", "ctx", None)
    return jax.shard_map(local, mesh=mesh, in_specs=in_specs, out_specs=out_specs, check_vma=False)
```

profile of v0, /device:TPU:0, one launch (start us, length us, event | category | flops | bytes accessed | tf_op | source)
XLA Modules:
  0.0 315.3 jit_solution(8348671642081136777)
XLA Ops:
  6.5 1.5 fusion.51
  13.4 3.4 %bitcast_select_fusion.2 = (bf16[128,4096]{1,0:T(8,128)(2,1)}, bf16[1,128,4096]{2,1,0:T(8,128)(2,1)}, bf16[1,128,4096]{2,1,0:T(8,128)(2,1)}) fusion(bf16[1,128,4096]{2,1,0:T(8,128)(2,1)} %param.7, bf16[1,128,4096]{2,1,0:T(8,128)(2,1)} %param.8, pred[]{:T(512)S(6)} %eq.24, pred[]{:T(512)S(6)} %lt.35, pred[]{:T(512)S(6)} %eq.25, pred[]{:T(512)S(6)} %lt.37, ...), kind=kLoop, calls=%fused_computation.48 | loop fusion | flops 2621440 | bytes 5242885 | tf_op jit(solution)/shard_map/jit(_where)/select_n | solution.py:73
  16.8 0.5 collective-permute-start
  18.1 0.6 multiply_reduce_fusion.1
  18.9 0.9 multiply_convert_fusion.1
  19.8 100.6 %all-reduce.7.cloned.1.call-done = (bf16[1,128,4096]{2,1,0:T(8,128)(2,1)}, bf16[1,128,4096]{2,1,0:T(8,128)(2,1)}) async-done(((bf16[1,128,4096]{2,1,0:T(8,128)(2,1)}, bf16[1,128,4096]{2,1,0:T(8,128)(2,1)}), (bf16[1,128,4096]{2,1,0:T(8,128)(2,1)}, bf16[1,128,4096]{2,1,0:T(8,128)(2,1)})) %all-reduce.7.cloned.1.call-update) | async-done | bytes 2097168 | tf_op jit(solution)/shard_map/psum | solution.py:23
  120.5 2.1 pad_maximum_fusion
  122.6 3.2 %copy.28 = bf16[64,8,32,128]{3,2,1,0:T(8,128)(2,1)} copy(bf16[64,8,32,128]{3,1,2,0:T(8,128)(2,1)S(1)} %bitcast.77) | data formatting | bytes 8388608
  125.8 7.6 %copy.26 = bf16[512,32,128]{0,2,1:T(8,128)(2,1)} copy(bf16[512,32,128]{2,1,0:T(8,128)(2,1)} %bitcast.79) | data formatting | bytes 8388608 | tf_op jit(solution)/shard_map/reshape;reshape | solution.py:43
  133.4 3.3 %fusion = f32[512,32]{0,1:T(8,128)S(1)} fusion(bf16[512,32,128]{0,2,1:T(8,128)(2,1)} %copy.26), kind=kLoop, calls=%fused_computation.4 | loop fusion | flops 6275072 | bytes 4259840 | tf_op jit(solution)/shard_map/reduce_sum | solution.py:34
  136.8 2.7 select_reduce_fusion.1
  139.5 2.2 fusion.6
  141.7 3.3 %bitcast_divide_fusion.1 = f32[128,32,128]{0,2,1:T(8,128)} fusion(bf16[512,32,128]{0,2,1:T(8,128)(2,1)S(1)} %copy-done.2, f32[32,128,512]{2,1,0:T(8,128)S(1)} %get-tuple-element.22, f32[32,128]{1,0:T(8,128)S(1)} %get-tuple-element.21, pred[128,512]{1,0:T(8,128)(4,1)S(1)} %fusion.45, f32[128,32]{0,1:T(8,128)S(1)} %bitcast.89), kind=kOutput, calls=%fused_computation.38 | convolution fusion | flops 543686656 | bytes 14778368 | tf_op jit(solution)/shard_map/hqk,khd->qhd/dot_general | solution.py:56
  145.1 1.9 copy.19
  147.0 1.2 add_convert_fusion
  148.3 3.4 %collective-permute-start.1 = (bf16[128,4096]{1,0:T(8,128)(2,1)}, bf16[128,4096]{1,0:T(8,128)(2,1)S(1)}, u32[]{:S(2)}, u32[]{:S(2)}) collective-permute-start(bf16[128,4096]{1,0:T(8,128)(2,1)} %add_convert_fusion), channel_id=1, source_target_pairs={{0,16},{1,17},{2,18},{3,19},{4,20},{5,21},{6,22},{7,23},{8,24},{9,... | collective-permute-start | bytes 3145736 | tf_op jit(solution)/shard_map/ppermute | solution.py:29
  151.7 21.8 %collective-permute-done.1 = bf16[128,4096]{1,0:T(8,128)(2,1)S(1)} collective-permute-done((bf16[128,4096]{1,0:T(8,128)(2,1)}, bf16[128,4096]{1,0:T(8,128)(2,1)S(1)}, u32[]{:S(2)}, u32[]{:S(2)}) %collective-permute-start.1) | collective-permute-done | bytes 1048608 | tf_op jit(solution)/shard_map/ppermute | solution.py:29
  173.5 2.8 convert_bitcast_fusion
  176.3 1.5 bitcast_select_fusion.5
  178.1 2.0 copy.31
  180.0 0.6 multiply_reduce_fusion
  180.7 0.9 multiply_convert_fusion
  181.6 96.6 %all-reduce.5.cloned.1.call-done = (bf16[1,128,4096]{2,1,0:T(8,128)(2,1)}, bf16[1,128,4096]{2,1,0:T(8,128)(2,1)}) async-done(((bf16[1,128,4096]{2,1,0:T(8,128)(2,1)}, bf16[1,128,4096]{2,1,0:T(8,128)(2,1)}), (bf16[1,128,4096]{2,1,0:T(8,128)(2,1)}, bf16[1,128,4096]{2,1,0:T(8,128)(2,1)})) %all-reduce.5.cloned.1.call-update) | async-done | bytes 2097168 | tf_op jit(solution)/shard_map/psum | solution.py:23
  278.2 2.1 pad_maximum_fusion.1
  280.3 3.2 %copy.30 = bf16[64,8,32,128]{3,2,1,0:T(8,128)(2,1)} copy(bf16[64,8,32,128]{3,1,2,0:T(8,128)(2,1)S(1)} %bitcast.78) | data formatting | bytes 8388608
  283.5 7.6 %copy.27 = bf16[512,32,128]{0,2,1:T(8,128)(2,1)} copy(bf16[512,32,128]{2,1,0:T(8,128)(2,1)} %bitcast.80) | data formatting | bytes 8388608 | tf_op jit(solution)/shard_map/reshape;reshape | solution.py:43
  291.1 3.3 %fusion.3 = f32[512,32]{0,1:T(8,128)S(1)} fusion(bf16[512,32,128]{0,2,1:T(8,128)(2,1)} %copy.27), kind=kLoop, calls=%fused_computation.7 | loop fusion | flops 6275072 | bytes 4259840 | tf_op jit(solution)/shard_map/reduce_sum | solution.py:34
  294.5 2.7 select_reduce_fusion
  297.2 2.2 fusion.8
  299.5 3.3 %bitcast_divide_fusion = f32[128,32,128]{0,2,1:T(8,128)} fusion(bf16[512,32,128]{0,2,1:T(8,128)(2,1)S(1)} %copy-done.1, f32[32,128,512]{2,1,0:T(8,128)S(1)} %get-tuple-element.24, f32[32,128]{1,0:T(8,128)S(1)} %get-tuple-element.23, pred[128,512]{1,0:T(8,128)(4,1)S(1)} %fusion.45, f32[128,32]{0,1:T(8,128)S(1)} %bitcast.88), kind=kOutput, calls=%fused_computation.37 | convolution fusion | flops 543686656 | bytes 14778368 | tf_op jit(solution)/shard_map/hqk,khd->qhd/dot_general | solution.py:56
  302.8 2.9 copy.23
  305.7 2.8 fusion.33
  (31 shorter events, 1.6 us)
Async XLA Ops:
  6.5 10.8 %copy-start = (bf16[1,128,4096]{2,1,0:T(8,128)(2,1)S(1)}, bf16[1,128,4096]{2,1,0:T(8,128)(2,1)}, u32[]{:S(2)}) copy-start(bf16[1,128,4096]{2,1,0:T(8,128)(2,1)} %param.8) | copy-start | bytes 3145732
  6.5 113.9 %all-reduce.7.cloned.1.call-start = ((), (), s32[]{:S(2)}) async-start(), calls=%async_computation.1 | async-start | bytes 4194304 | tf_op jit(solution)/shard_map/psum | solution.py:23
  13.4 4.2 %copy-start.5 = (s32[16,4]{0,1:T(4,128)S(1)}, s32[16,4]{0,1:T(4,128)}, u32[]{:S(2)}) copy-start(s32[16,4]{0,1:T(4,128)} %param.10) | copy-start | bytes 772
  16.8 103.7 %collective-permute-start = (bf16[128,4096]{1,0:T(8,128)(2,1)}, bf16[128,4096]{1,0:T(8,128)(2,1)}, u32[]{:S(2)}, u32[]{:S(2)}) collective-permute-start(bf16[128,4096]{1,0:T(8,128)(2,1)} %get-tuple-element.16), channel_id=1, source_target_pairs={{0,1},{1,2},{2,3},{3,4},{4,5},{5,6},{6,7},{7,8},{8,9},{9,10},{10,1... | collective-permute-start | bytes 3145736 | tf_op jit(solution)/shard_map/ppermute | solution.py:18
  17.3 260.9 %all-reduce.5.cloned.1.call-start = ((), (), s32[]{:S(2)}) async-start(), calls=%async_computation | async-start | bytes 4194304 | tf_op jit(solution)/shard_map/psum | solution.py:23
  17.3 1.6 copy-start.3
  133.4 3.4 %copy-start.2 = (bf16[512,32,128]{0,2,1:T(8,128)(2,1)S(1)}, bf16[512,32,128]{0,2,1:T(8,128)(2,1)}, u32[]{:S(2)}) copy-start(bf16[512,32,128]{0,2,1:T(8,128)(2,1)} %copy.26) | copy-start | bytes 12582916
  133.4 3.4 %copy-start.6 = (f32[1,4096]{1,0:T(1,128)S(1)}, f32[1,4096]{1,0:T(1,128)}, u32[]{:S(2)}) copy-start(f32[1,4096]{1,0:T(1,128)} %param.12) | copy-start | bytes 49156
  145.1 1.9 copy-start.4
  148.3 25.2 %collective-permute-start.1 = (bf16[128,4096]{1,0:T(8,128)(2,1)}, bf16[128,4096]{1,0:T(8,128)(2,1)S(1)}, u32[]{:S(2)}, u32[]{:S(2)}) collective-permute-start(bf16[128,4096]{1,0:T(8,128)(2,1)} %add_convert_fusion), channel_id=1, source_target_pairs={{0,16},{1,17},{2,18},{3,19},{4,20},{5,21},{6,22},{7,23},{8,24},{9,... | collective-permute-start | bytes 3145736 | tf_op jit(solution)/shard_map/ppermute | solution.py:29
  177.8 100.4 %collective-permute-start.2 = (bf16[128,4096]{1,0:T(8,128)(2,1)S(1)}, bf16[128,4096]{1,0:T(8,128)(2,1)}, u32[]{:S(2)}, u32[]{:S(2)}) collective-permute-start(bf16[128,4096]{1,0:T(8,128)(2,1)S(1)} %get-tuple-element.13), channel_id=1, source_target_pairs={{0,1},{1,2},{2,3},{3,4},{4,5},{5,6},{6,7},{7,8},{8,9},{9,10},{10,1... | collective-permute-start | bytes 3145736 | tf_op jit(solution)/shard_map/ppermute | solution.py:18
  291.1 3.4 %copy-start.1 = (bf16[512,32,128]{0,2,1:T(8,128)(2,1)S(1)}, bf16[512,32,128]{0,2,1:T(8,128)(2,1)}, u32[]{:S(2)}) copy-start(bf16[512,32,128]{0,2,1:T(8,128)(2,1)} %copy.27) | copy-start | bytes 12582916
Sparse Core Ops, SparseCore 0:
  17.4 103.0 all-reduce.6
  178.0 100.2 all-reduce.4
where the time goes:
time: 316 us; the launch traced here: 315 us
  waiting for transfers between devices  219 us (69%)
  local copies, waits for them, and re-layouts  30.5 us (10%)
  other arithmetic  30.5 us (10%)
  between operations  19 us (6%)
  matrix products  12 us (4%)
  starting transfers between devices  4.18 us (1%)
    psum x2, waiting for transfers between devices, broadcast(): return lax.psum(kept, axis)  197 us
    ppermute x1, waiting for transfers between devices, passed_along(): lax.ppermute(value, axis, [(source, source + steps) for source in range(i...  21.8 us
    another operation x2, local copies, waits for them, and re-layouts, attend_block(): values = key_flat.reshape(NSEL * BLOCK, HEADS, HD)  15.1 us
    unnamed x18, local copies, waits for them, and re-layouts  9.06 us
    reduce_sum x4, other arithmetic, normalize(): jnp.mean(widened * widened, axis=-1, keepdims=True) + 1e-06  7.74 us
    dot_general x2, matrix products, attend_block(): jnp.einsum('hqk,khd->qhd', weights, values, preferred_element_type=jnp.fl...  6.68 us
  transfers between devices with their start and end apart: 5, of which 3 were waited for; matrix products, arithmetic and copies ran while one was open for 2% of the time, Pallas kernels for 0%

commit v1 on v0

v1 whole, which is shorter than its diff:
```python
import functools

import jax
import jax.numpy as jnp
from jax import lax
from jax.experimental import pallas as pl
from jax.experimental.pallas import tpu as pltpu
from jax.sharding import PartitionSpec as P

HEADS = 32
HD = 128
BLOCK = 128
LOCAL = 2
WIDTH = 4096
CHUNKS = 4
CHUNK = WIDTH // CHUNKS
HALF = CHUNK // 2
OUTER = 4
MESH = pl.DeviceIdType.MESH

A_S, A_R, YR_S, YR_R, YL_S, YL_R, ZR_S, ZR_R, ZL_S, ZL_R, C_S, C_R = range(12)
ROWS = 12


def kernel(
    n, sections, r_ref, early_ref, cur_ref, next_ref, gq_ref, gk_ref, go_ref, out_ref,
    second, first, prev, res, abuf, ycand, yfl, yfr, ysr, ysl, zcand, zfl, zfr, zsr, zsl,
    sems, psems, hsems,
):
    inner = n // (2 * OUTER)
    p = lax.axis_index("ctx")
    s = lax.axis_index("section")
    core = p % 2
    peer = p + 1 - 2 * core
    yi = (p // 2) % inner
    zi = p // (2 * inner)
    ystride, zstride = 2, 2 * inner
    after, before = lax.rem(p + 1, n), lax.rem(p + n - 1, n)
    r = r_ref[0]
    rc, ry, rz = r % 2, (r // 2) % inner, r // (2 * inner)
    later_ok = r + LOCAL <= p
    sends = s < sections - 1
    is_last = p == n - 1

    barrier = pltpu.get_barrier_semaphore()

    def greet(target):
        pl.semaphore_signal(barrier, inc=1, device_id=target, device_id_type=MESH)

    greet({"ctx": peer})
    greet({"ctx": after})
    greet({"ctx": before})
    total = jnp.int32(3)
    for there, axis, target in (
        (yi > 0, "ctx", p - ystride), (yi < inner - 1, "ctx", p + ystride),
        (zi > 0, "ctx", p - zstride), (zi < OUTER - 1, "ctx", p + zstride),
        (s > 0, "section", s - 1), (s < sections - 1, "section", s + 1),
    ):
        @pl.when(there)
        def _(axis=axis, target=target):
            greet({axis: target})
        total = total + there.astype(jnp.int32)
    pl.semaphore_wait(barrier, total)

    def cols(k):
        return pl.ds(pl.multiple_of(k * CHUNK, CHUNK), CHUNK)

    def half(k, c):
        return pl.ds(pl.multiple_of(k * CHUNK + c * HALF, HALF), HALF)

    def remote(src, dst, send, recv, target):
        return pltpu.make_async_remote_copy(
            src_ref=src, dst_ref=dst, send_sem=send, recv_sem=recv,
            device_id=target, device_id_type=MESH,
        )

    def swap_in(b, k, src):
        return remote(src.at[:, half(k, 1 - core)], abuf.at[b, k],
                      sems.at[A_S, b, k], sems.at[A_R, b, k], {"ctx": peer})

    def swap_out(b, k):
        part = res.at[b, :, half(k, core)]
        return remote(part, part, sems.at[C_S, b, k], sems.at[C_R, b, k], {"ctx": peer})

    def behind(b, k, src):
        return remote(src.at[:, cols(k)], prev.at[b, :, cols(k)],
                      psems.at[0, b, k], psems.at[1, b, k], {"ctx": after})

    def handoff(k):
        return remote(first.at[:, cols(k)], second.at[:, cols(k)],
                      hsems.at[0, k], hsems.at[1, k], {"section": lax.rem(s + 1, sections)})

    class Chain:
        def __init__(self, j, length, t, stride, cand, fl, fr, sr, sl, row):
            self.j, self.length, self.t, self.stride = j, length, t, stride
            self.cand, self.fl, self.fr, self.sr, self.sl, self.row = cand, fl, fr, sr, sl, row

        def right(self, b, k, src):
            return remote(src.at[b, k], self.fl.at[b, k], sems.at[self.row, b, k],
                          sems.at[self.row + 1, b, k], {"ctx": lax.rem(p + self.stride, n)})

        def left(self, b, k, src):
            return remote(src.at[b, k], self.fr.at[b, k], sems.at[self.row + 2, b, k],
                          sems.at[self.row + 3, b, k], {"ctx": lax.rem(p + n - self.stride, n)})

        def begin(self, b, k):
            @pl.when(self.j == 0)
            def _():
                self.right(b, k, self.cand).start()

            @pl.when(self.j == self.length - 1)
            def _():
                self.left(b, k, self.cand).start()

        def go_right(self, b, k):
            self.right(b, k, self.cand).wait_recv()

            @pl.when(self.j < self.length - 1)
            def _():
                self.sr[b, k] = jnp.where(self.t < self.j, self.fl[b, k], self.cand[b, k])
                self.right(b, k, self.sr).start()

        def go_left(self, b, k):
            self.left(b, k, self.cand).wait_recv()

            @pl.when(self.j > 0)
            def _():
                self.sl[b, k] = jnp.where(self.t > self.j, self.fr[b, k], self.cand[b, k])
                self.left(b, k, self.sl).start()

        def relay(self, b, k, store):
            j, t = self.j, self.t
            low = j < self.length // 2

            @pl.when(low)
            def _():
                @pl.when(j > 0)
                def _():
                    self.go_right(b, k)
                self.go_left(b, k)

            @pl.when(jnp.logical_not(low))
            def _():
                @pl.when(j < self.length - 1)
                def _():
                    self.go_left(b, k)
                self.go_right(b, k)

            @pl.when(j == 0)
            def _():
                store(jnp.where(t > j, self.fr[b, k], self.cand[b, k]))

            @pl.when(j == self.length - 1)
            def _():
                store(jnp.where(t < j, self.fl[b, k], self.cand[b, k]))

            @pl.when((j > 0) & (j < self.length - 1))
            def _():
                kept = jnp.where(t > j, self.fr[b, k], self.cand[b, k])
                store(jnp.where(t < j, self.fl[b, k], kept))

        def drain(self, b, k):
            @pl.when(self.j < self.length - 1)
            def _():
                self.right(b, k, self.cand).wait_send()

            @pl.when(self.j > 0)
            def _():
                self.left(b, k, self.cand).wait_send()

    ychain = Chain(yi, inner, ry, ystride, ycand, yfl, yfr, ysr, ysl, YR_S)
    zchain = Chain(zi, OUTER, rz, zstride, zcand, zfl, zfr, zsr, zsl, ZR_S)

    def stage_select(b, k, src):
        swap_in(b, k, src).wait_recv()
        ycand[b, k] = jnp.where(rc == core, src[:, half(k, core)], abuf[b, k])
        ychain.begin(b, k)

    def stage_y(b, k):
        def store(value):
            zcand[b, k] = value
        ychain.relay(b, k, store)
        zchain.begin(b, k)

    def stage_z(b, k):
        def store(value):
            res[b, :, half(k, core)] = value
        zchain.relay(b, k, store)
        swap_out(b, k).start()

    def drain(b, k, src):
        swap_in(b, k, src).wait_send()
        ychain.drain(b, k)
        zchain.drain(b, k)
        swap_out(b, k).wait_send()

    causal = (lax.broadcasted_iota(jnp.int32, (BLOCK, BLOCK), 1)
              <= lax.broadcasted_iota(jnp.int32, (BLOCK, BLOCK), 0))

    def normed(rows):
        wide = rows.astype(jnp.float32)
        return wide * lax.rsqrt(jnp.mean(wide * wide, axis=-1, keepdims=True) + 1e-06)

    def attend(k, query_ref, before_at, early_at, later_at, to_ref):
        def head(h, carry):
            at = pl.ds(pl.multiple_of(k * CHUNK + h * HD, HD), HD)
            gk = gk_ref[:, at]
            own = query_ref[:, at]
            rest = [prev[before_at, :, at], res[early_at, :, at], res[later_at, :, at]]
            own_n = normed(own)
            q = (own_n * gq_ref[:, at] * HD ** (-0.5)).astype(jnp.bfloat16)
            keys = [(own_n * gk).astype(jnp.bfloat16)]
            keys += [(normed(x) * gk).astype(jnp.bfloat16) for x in rest]
            keys = jnp.concatenate(keys, axis=0)
            values = jnp.concatenate([own] + rest, axis=0)
            sc = lax.dot_general(q, keys, (((1,), (1,)), ((), ())),
                                 preferred_element_type=jnp.float32)
            s0 = jnp.where(causal, sc[:, :BLOCK], -jnp.inf)
            s1 = sc[:, BLOCK:2 * BLOCK]
            s2 = sc[:, 2 * BLOCK:3 * BLOCK]
            s3 = jnp.where(later_ok, sc[:, 3 * BLOCK:], -jnp.inf)
            top = jnp.max(jnp.maximum(jnp.maximum(s0, s1), jnp.maximum(s2, s3)),
                          axis=-1, keepdims=True)
            raw = [jnp.exp(x - top) for x in (s0, s1, s2, s3)]
            tot = jnp.sum((raw[0] + raw[1]) + (raw[2] + raw[3]), axis=-1, keepdims=True)
            weights = jnp.concatenate([x.astype(jnp.bfloat16) for x in raw], axis=1)
            context = jnp.dot(weights, values, preferred_element_type=jnp.float32)
            to_ref[:, at] = (own.astype(jnp.float32)
                             + go_ref[:, at] * (context / tot)).astype(jnp.bfloat16)
            return carry
        lax.fori_loop(0, CHUNK // HD, head, 0)

    def each(count, body):
        def step(k, carry):
            body(k)
            return carry
        lax.fori_loop(0, count, step, 0)

    def staged(lag, t, body):
        k = t - lag

        @pl.when((k >= 0) & (k < CHUNKS))
        def _():
            body(jnp.clip(k, 0, CHUNKS - 1))

    def open_first(k):
        @pl.when(sends)
        def _():
            swap_in(0, k, early_ref).start()
        swap_in(1, k, cur_ref).start()

        @pl.when(sends & is_last)
        def _():
            behind(0, k, early_ref).start()

        @pl.when(sends & jnp.logical_not(is_last))
        def _():
            behind(0, k, cur_ref).start()

        @pl.when(s == 0)
        def _():
            second[:, cols(k)] = next_ref[:, cols(k)]

    each(CHUNKS, open_first)

    def both(stage, k, *src):
        @pl.when(sends)
        def _():
            stage(0, k, *src[:1])
        stage(1, k, *src[1:])

    def finish_first(k):
        swap_out(1, k).wait_recv()

        @pl.when(sends)
        def _():
            swap_out(0, k).wait_recv()
            behind(0, k, cur_ref).wait_recv()
            attend(k, cur_ref, 0, 0, 1, first)
            handoff(k).start()

    def first_step(t):
        staged(0, t, lambda k: both(stage_select, k, early_ref, cur_ref))
        staged(1, t, lambda k: both(stage_y, k))
        staged(2, t, lambda k: both(stage_z, k))
        staged(3, t, finish_first)

    each(CHUNKS + 3, first_step)

    def open_second(k):
        @pl.when(s > 0)
        def _():
            handoff(k).wait_recv()
        swap_in(2, k, second).start()

        @pl.when(is_last)
        def _():
            behind(1, k, cur_ref).start()

        @pl.when(jnp.logical_not(is_last))
        def _():
            behind(1, k, second).start()

    def finish_second(k):
        swap_out(2, k).wait_recv()
        behind(1, k, second).wait_recv()
        attend(k, second, 1, 1, 2, out_ref)

    def second_step(t):
        staged(0, t, open_second)
        staged(1, t, lambda k: stage_select(2, k, second))
        staged(2, t, lambda k: stage_y(2, k))
        staged(3, t, lambda k: stage_z(2, k))
        staged(4, t, finish_second)

    each(CHUNKS + 4, second_step)

    def close(k):
        @pl.when(sends)
        def _():
            drain(0, k, early_ref)
            behind(0, k, cur_ref).wait_send()
            handoff(k).wait_send()
        drain(1, k, cur_ref)
        drain(2, k, second)
        behind(1, k, second).wait_send()

    each(CHUNKS, close)


def local(earlier_span, span_inputs, next_inputs, block_list, q_gain, k_gain, out_gain):
    n = lax.axis_size("ctx")
    sections = lax.axis_size("section")
    r = lax.dynamic_slice(block_list, (n - 1, LOCAL), (1, 1)).reshape(1)
    piece = (3, CHUNKS, BLOCK, HALF)
    vmem = pl.BlockSpec(memory_space=pltpu.VMEM)
    result = pl.pallas_call(
        functools.partial(kernel, n, sections),
        out_shape=jax.ShapeDtypeStruct((BLOCK, WIDTH), jnp.bfloat16),
        in_specs=[pl.BlockSpec(memory_space=pltpu.SMEM)] + [vmem] * 6,
        out_specs=vmem,
        scratch_shapes=[
            pltpu.VMEM((BLOCK, WIDTH), jnp.bfloat16),
            pltpu.VMEM((BLOCK, WIDTH), jnp.bfloat16),
            pltpu.VMEM((2, BLOCK, WIDTH), jnp.bfloat16),
            pltpu.VMEM((3, BLOCK, WIDTH), jnp.bfloat16),
        ] + [pltpu.VMEM(piece, jnp.bfloat16)] * 11 + [
            pltpu.SemaphoreType.DMA((ROWS, 3, CHUNKS)),
            pltpu.SemaphoreType.DMA((2, 2, CHUNKS)),
            pltpu.SemaphoreType.DMA((2, CHUNKS)),
        ],
        compiler_params=pltpu.CompilerParams(
            collective_id=0, has_side_effects=True, vmem_limit_bytes=48 * 1024 * 1024,
        ),
    )(r, earlier_span[0], span_inputs[0], next_inputs, q_gain, k_gain, out_gain)
    return result[None]


def solution(mesh):
    in_specs = (
        P("section", "ctx", None),
        P("section", "ctx", None),
        P("ctx", None),
        P(),
        P("section", None),
        P("section", None),
        P("section", None),
    )
    out_specs = P("section", "ctx", None)
    return jax.shard_map(local, mesh=mesh, in_specs=in_specs, out_specs=out_specs, check_vma=False)
```

time: 316 us -> 149 us (0.47)
  waiting for transfers between devices: 219 us -> 0 us
  Pallas kernels: 0 us -> 140 us
  other arithmetic: 30.5 us -> 0 us
  local copies, waits for them, and re-layouts: 30.5 us -> 8.06 us
  between operations: 19 us -> 0.02 us
  matrix products: 12 us -> 0 us
  starting transfers between devices: 4.18 us -> 0 us
    psum x2 -> x0, waiting for transfers between devices: 197 us -> none  [broadcast(): return lax.psum(kept, axis)]
    pallas_call x0 -> x1, Pallas kernels: none -> 140 us  [local(): pl.pallas_call(functools.partial(kernel, n, sections), out_shape=jax.Shap...]
    ppermute x3 -> x0, waiting for transfers between devices: 21.8 us -> none  [the longest x1 21.8 us: passed_along(): lax.ppermute(value, axis, [(source, source + steps) for source in range(i...]
    another operation x2 -> x0, local copies, waits for them, and re-layouts: 15.1 us -> none  [attend_block(): values = key_flat.reshape(NSEL * BLOCK, HEADS, HD)]
    reduce_sum x6 -> x0, other arithmetic: 12.2 us -> none  [the longest x4 7.74 us: normalize(): jnp.mean(widened * widened, axis=-1, keepdims=True) + 1e-06]
    dot_general x4 -> x0, matrix products: 12 us -> none  [the longest x2 6.68 us: attend_block(): jnp.einsum('hqk,khd->qhd', weights, values, preferred_element_type=jnp.fl...]
    select_n x3 -> x0, other arithmetic: 4.95 us -> none  [the longest x2 4.95 us: previous(): payload = jnp.where(position == group_size - 1, earlier_rows, current_rows)]
    reshape x2 -> x0, local copies, waits for them, and re-layouts: 4.81 us -> none  [attend_block(): (context / jnp.transpose(totals)[:, :, None]).reshape(BLOCK, WIDTH)]
  transfers between devices with their start and end apart: 5 -> 0, of which waited for: 3 -> 0; matrix products, arithmetic and copies ran while one was open for 2% -> 0% of each run, Pallas kernels for 0% -> 0%
where the time goes in v1:
time: 149 us; the launch traced here: 148 us
  Pallas kernels  140 us (94%)
  local copies, waits for them, and re-layouts  8.06 us (5%)
    pallas_call x1, Pallas kernels, local(): pl.pallas_call(functools.partial(kernel, n, sections), out_shape=jax.Shap...  140 us
    unnamed x13, local copies, waits for them, and re-layouts  6.8 us

profile of v1, /device:TPU:0, one launch (start us, length us, event | category | flops | bytes accessed | tf_op | source)
XLA Modules:
  0.0 148.1 jit_solution(7671360062733676675)
XLA Ops:
  0.0 1.3 dynamic_slice.3
  1.3 0.0 copy-start
  1.3 1.2 copy-done
  2.5 0.0 copy-start.1
  2.5 1.2 copy-done.1
  3.7 0.0 copy-start.2
  3.7 1.2 copy-done.2
  4.9 0.0 copy-start.3
  4.9 0.7 copy-done.3
  5.7 0.0 copy-start.4
  5.7 0.7 copy-done.4
  6.4 0.0 copy-start.5
  6.4 0.7 copy-done.5
  7.1 140.0 %shard_map.73 = bf16[128,4096]{1,0:T(8,128)(2,1)S(1)} custom-call(s32[1]{0:T(128)} %bitcast.r_ref, bf16[128,4096]{1,0:T(8,128)(2,1)S(1)} %bitcast.5, bf16[128,4096]{1,0:T(8,128)(2,1)S(1)} %bitcast.6, bf16[128,4096]{1,0:T(8,128)(2,1)S(1)} %copy-done.2, f32[1,4096]{1,0:T(1,128)S(1)} %copy-done.3, f32[1,4096]{1,0:T(1,128)S(1)} %copy-done.4, f32[1,4096]{1,0:T(1,128)S(1)} %copy-done.5), custom_call_target="tpu_custom_call" | custom-call | tf_op jit(solution)/shard_map/pallas_call | solution.py:337
  147.1 1.0 copy.9
Async XLA Ops:
  1.3 1.2 copy-start
  2.5 1.2 copy-start.1
  3.7 1.2 copy-start.2
  4.9 0.7 copy-start.3
  5.7 0.7 copy-start.4
  6.4 0.7 copy-start.5

commit v2 on v1

--- a/solution.py
+++ b/solution.py
@@ -12,7 +12,8 @@
 BLOCK = 128
 LOCAL = 2
 WIDTH = 4096
-CHUNKS = 4
+CHUNKS = 16
+LAG = 2
 CHUNK = WIDTH // CHUNKS
 HALF = CHUNK // 2
 OUTER = 4
@@ -23,9 +24,9 @@
 
 
 def kernel(
-    n, sections, r_ref, early_ref, cur_ref, next_ref, gq_ref, gk_ref, go_ref, out_ref,
-    second, first, prev, res, abuf, ycand, yfl, yfr, ysr, ysl, zcand, zfl, zfr, zsr, zsl,
-    sems, psems, hsems,
+    n, sections, list_ref, early_in, cur_in, next_in, gq_ref, gk_ref, go_ref, out_ref,
+    early_ref, cur_ref, second, first, prev, res, abuf, ycand, yfl, yfr, ysr, ysl, zcand, zfl, zfr, zsr, zsl,
+    sems, psems, hsems, lsems,
 ):
     inner = n // (2 * OUTER)
     p = lax.axis_index("ctx")
@@ -36,11 +37,21 @@
     zi = p // (2 * inner)
     ystride, zstride = 2, 2 * inner
     after, before = lax.rem(p + 1, n), lax.rem(p + n - 1, n)
-    r = r_ref[0]
+    r = list_ref[n - 1, LOCAL]
     rc, ry, rz = r % 2, (r // 2) % inner, r // (2 * inner)
     later_ok = r + LOCAL <= p
     sends = s < sections - 1
     is_last = p == n - 1
+
+    fetch_early = pltpu.make_async_copy(early_in.at[0], early_ref, lsems.at[0])
+    fetch_cur = pltpu.make_async_copy(cur_in.at[0], cur_ref, lsems.at[1])
+    fetch_next = pltpu.make_async_copy(next_in, second, lsems.at[2])
+    fetch_early.start()
+    fetch_cur.start()
+
+    @pl.when(s == 0)
+    def _():
+        fetch_next.start()
 
     barrier = pltpu.get_barrier_semaphore()
 
@@ -61,6 +72,8 @@
             greet({axis: target})
         total = total + there.astype(jnp.int32)
     pl.semaphore_wait(barrier, total)
+    fetch_early.wait()
+    fetch_cur.wait()
 
     def cols(k):
         return pl.ds(pl.multiple_of(k * CHUNK, CHUNK), CHUNK)
@@ -90,6 +103,19 @@
         return remote(first.at[:, cols(k)], second.at[:, cols(k)],
                       hsems.at[0, k], hsems.at[1, k], {"section": lax.rem(s + 1, sections)})
 
+    def each(count, body):
+        def step(k, carry):
+            body(k)
+            return carry
+        lax.fori_loop(0, count, step, 0)
+
+    def staged(lag, t, body):
+        k = t - lag
+
+        @pl.when((k >= 0) & (k < CHUNKS))
+        def _():
+            body(jnp.clip(k, 0, CHUNKS - 1))
+
     class Chain:
         def __init__(self, j, length, t, stride, cand, fl, fr, sr, sl, row):
             self.j, self.length, self.t, self.stride = j, length, t, stride
@@ -114,50 +140,48 @@
 
         def go_right(self, b, k):
             self.right(b, k, self.cand).wait_recv()
-
-            @pl.when(self.j < self.length - 1)
-            def _():
-                self.sr[b, k] = jnp.where(self.t < self.j, self.fl[b, k], self.cand[b, k])
-                self.right(b, k, self.sr).start()
+            self.sr[b, k] = jnp.where(self.t < self.j, self.fl[b, k], self.cand[b, k])
+            self.right(b, k, self.sr).start()
 
         def go_left(self, b, k):
             self.left(b, k, self.cand).wait_recv()
-
-            @pl.when(self.j > 0)
-            def _():
-                self.sl[b, k] = jnp.where(self.t > self.j, self.fr[b, k], self.cand[b, k])
-                self.left(b, k, self.sl).start()
-
-        def relay(self, b, k, store):
-            j, t = self.j, self.t
-            low = j < self.length // 2
-
-            @pl.when(low)
-            def _():
-                @pl.when(j > 0)
+            self.sl[b, k] = jnp.where(self.t > self.j, self.fr[b, k], self.cand[b, k])
+            self.left(b, k, self.sl).start()
+
+        def relay(self, t, lag, items):
+            j, last = self.j, self.length - 1
+            inside = (j > 0) & (j < last)
+
+            def run(go):
+                def body(k):
+                    for there, b in items:
+                        @pl.when(there & inside)
+                        def _(b=b):
+                            go(b, k)
+                return body
+
+            if self.length > 2:
+                staged(lag + j * LAG, t, run(self.go_right))
+                staged(lag + (last - j) * LAG, t, run(self.go_left))
+
+        def finish(self, b, k, store):
+            j, t, last = self.j, self.t, self.length - 1
+
+            @pl.when(j == 0)
+            def _():
+                self.left(b, k, self.cand).wait_recv()
+                store(jnp.where(t > j, self.fr[b, k], self.cand[b, k]))
+
+            @pl.when(j == last)
+            def _():
+                self.right(b, k, self.cand).wait_recv()
+                store(jnp.where(t < j, self.fl[b, k], self.cand[b, k]))
+
+            if last > 1:
+                @pl.when((j > 0) & (j < last))
                 def _():
-                    self.go_right(b, k)
-                self.go_left(b, k)
-
-            @pl.when(jnp.logical_not(low))
-            def _():
-                @pl.when(j < self.length - 1)
-                def _():
-                    self.go_left(b, k)
-                self.go_right(b, k)
-
-            @pl.when(j == 0)
-            def _():
-                store(jnp.where(t > j, self.fr[b, k], self.cand[b, k]))
-
-            @pl.when(j == self.length - 1)
-            def _():
-                store(jnp.where(t < j, self.fl[b, k], self.cand[b, k]))
-
-            @pl.when((j > 0) & (j < self.length - 1))
-            def _():
-                kept = jnp.where(t > j, self.fr[b, k], self.cand[b, k])
-                store(jnp.where(t < j, self.fl[b, k], kept))
+                    kept = jnp.where(t > j, self.fr[b, k], self.cand[b, k])
+                    store(jnp.where(t < j, self.fl[b, k], kept))
 
         def drain(self, b, k):
             @pl.when(self.j < self.length - 1)
@@ -179,13 +203,13 @@
     def stage_y(b, k):
         def store(value):
             zcand[b, k] = value
-        ychain.relay(b, k, store)
+        ychain.finish(b, k, store)
         zchain.begin(b, k)
 
     def stage_z(b, k):
         def store(value):
             res[b, :, half(k, core)] = value
-        zchain.relay(b, k, store)
+        zchain.finish(b, k, store)
         swap_out(b, k).start()
 
     def drain(b, k, src):
@@ -228,20 +252,7 @@
             to_ref[:, at] = (own.astype(jnp.float32)
                              + go_ref[:, at] * (context / tot)).astype(jnp.bfloat16)
             return carry
-        lax.fori_loop(0, CHUNK // HD, head, 0)
-
-    def each(count, body):
-        def step(k, carry):
-            body(k)
-            return carry
-        lax.fori_loop(0, count, step, 0)
-
-    def staged(lag, t, body):
-        k = t - lag
-
-        @pl.when((k >= 0) & (k < CHUNKS))
-        def _():
-            body(jnp.clip(k, 0, CHUNKS - 1))
+        lax.fori_loop(0, CHUNK // HD, head, 0, unroll=min(4, CHUNK // HD))
 
     def open_first(k):
         @pl.when(sends)
@@ -257,11 +268,11 @@
         def _():
             behind(0, k, cur_ref).start()
 
-        @pl.when(s == 0)
-        def _():
-            second[:, cols(k)] = next_ref[:, cols(k)]
-
     each(CHUNKS, open_first)
+
+    @pl.when(s == 0)
+    def _():
+        fetch_next.wait()
 
     def both(stage, k, *src):
         @pl.when(sends)
@@ -279,14 +290,6 @@
             attend(k, cur_ref, 0, 0, 1, first)
             handoff(k).start()
 
-    def first_step(t):
-        staged(0, t, lambda k: both(stage_select, k, early_ref, cur_ref))
-        staged(1, t, lambda k: both(stage_y, k))
-        staged(2, t, lambda k: both(stage_z, k))
-        staged(3, t, finish_first)
-
-    each(CHUNKS + 3, first_step)
-
     def open_second(k):
         @pl.when(s > 0)
         def _():
@@ -304,16 +307,37 @@
     def finish_second(k):
         swap_out(2, k).wait_recv()
         behind(1, k, second).wait_recv()
-        attend(k, second, 1, 1, 2, out_ref)
-
-    def second_step(t):
-        staged(0, t, open_second)
-        staged(1, t, lambda k: stage_select(2, k, second))
-        staged(2, t, lambda k: stage_y(2, k))
-        staged(3, t, lambda k: stage_z(2, k))
-        staged(4, t, finish_second)
-
-    each(CHUNKS + 4, second_step)
+        attend(k, second, 1, 1, 2, out_ref.at[0])
+
+    spread = (inner - 1) * LAG
+    span = (OUTER - 1) * LAG
+    early_item = [(sends, 0), (s >= 0, 1)]
+    late_item = [(s >= 0, 2)]
+    first_y = spread
+    first_z = first_y + span
+    first_end = first_z + LAG
+    open_at = first_end + LAG
+    pick_at = open_at + 1
+    second_y = pick_at + spread
+    second_z = second_y + span
+    second_end = second_z + LAG
+
+    def step(t):
+        staged(0, t, lambda k: both(stage_select, k, early_ref, cur_ref))
+        ychain.relay(t, 0, early_item)
+        staged(first_y, t, lambda k: both(stage_y, k))
+        zchain.relay(t, first_y, early_item)
+        staged(first_z, t, lambda k: both(stage_z, k))
+        staged(open_at, t, open_second)
+        staged(pick_at, t, lambda k: stage_select(2, k, second))
+        ychain.relay(t, pick_at, late_item)
+        staged(second_y, t, lambda k: stage_y(2, k))
+        zchain.relay(t, second_y, late_item)
+        staged(second_z, t, lambda k: stage_z(2, k))
+        staged(first_end, t, finish_first)
+        staged(second_end, t, finish_second)
+
+    each(CHUNKS + second_end, step)
 
     def close(k):
         @pl.when(sends)
@@ -331,29 +355,26 @@
 def local(earlier_span, span_inputs, next_inputs, block_list, q_gain, k_gain, out_gain):
     n = lax.axis_size("ctx")
     sections = lax.axis_size("section")
-    r = lax.dynamic_slice(block_list, (n - 1, LOCAL), (1, 1)).reshape(1)
     piece = (3, CHUNKS, BLOCK, HALF)
     vmem = pl.BlockSpec(memory_space=pltpu.VMEM)
-    result = pl.pallas_call(
+    return pl.pallas_call(
         functools.partial(kernel, n, sections),
-        out_shape=jax.ShapeDtypeStruct((BLOCK, WIDTH), jnp.bfloat16),
-        in_specs=[pl.BlockSpec(memory_space=pltpu.SMEM)] + [vmem] * 6,
+        out_shape=jax.ShapeDtypeStruct((1, BLOCK, WIDTH), jnp.bfloat16),
+        in_specs=[pl.BlockSpec(memory_space=pltpu.SMEM)] + [pl.BlockSpec(memory_space=pl.ANY)] * 3 + [vmem] * 3,
         out_specs=vmem,
-        scratch_shapes=[
-            pltpu.VMEM((BLOCK, WIDTH), jnp.bfloat16),
-            pltpu.VMEM((BLOCK, WIDTH), jnp.bfloat16),
+        scratch_shapes=[pltpu.VMEM((BLOCK, WIDTH), jnp.bfloat16)] * 4 + [
             pltpu.VMEM((2, BLOCK, WIDTH), jnp.bfloat16),
             pltpu.VMEM((3, BLOCK, WIDTH), jnp.bfloat16),
         ] + [pltpu.VMEM(piece, jnp.bfloat16)] * 11 + [
             pltpu.SemaphoreType.DMA((ROWS, 3, CHUNKS)),
             pltpu.SemaphoreType.DMA((2, 2, CHUNKS)),
             pltpu.SemaphoreType.DMA((2, CHUNKS)),
+            pltpu.SemaphoreType.DMA((3,)),
         ],
         compiler_params=pltpu.CompilerParams(
             collective_id=0, has_side_effects=True, vmem_limit_bytes=48 * 1024 * 1024,
         ),
-    )(r, earlier_span[0], span_inputs[0], next_inputs, q_gain, k_gain, out_gain)
-    return result[None]
+    )(block_list, earlier_span, span_inputs, next_inputs, q_gain, k_gain, out_gain)
 
 
 def solution(mesh):

time: 149 us -> 101 us (0.68)
  Pallas kernels: 140 us -> 93.3 us
    pallas_call x1, Pallas kernels: 140 us -> 93.3 us  [local(): pl.pallas_call(functools.partial(kernel, n, sections), out_shape=jax.Shap...]
    unnamed x13 -> x14, local copies, waits for them, and re-layouts: 6.8 us -> 7.55 us
where the time goes in v2:
time: 101 us
  Pallas kernels  93.3 us (92%)
  local copies, waits for them, and re-layouts  7.55 us (7%)
    pallas_call x1, Pallas kernels, local(): pl.pallas_call(functools.partial(kernel, n, sections), out_shape=jax.Shap...  93.3 us
    unnamed x14, local copies, waits for them, and re-layouts  7.55 us

profile of v2, /device:TPU:0, one launch (start us, length us, event | category | flops | bytes accessed | tf_op | source)
XLA Modules:
  0.0 100.9 jit_solution(6184180614190733779)
XLA Ops:
  0.0 0.8 copy.8.list_ref
  0.8 0.0 copy-start
  0.8 1.2 %copy-done = bf16[1,128,4096]{2,1,0:T(8,128)(2,1)S(1)} copy-done((bf16[1,128,4096]{2,1,0:T(8,128)(2,1)S(1)}, bf16[1,128,4096]{2,1,0:T(8,128)(2,1)}, u32[]{:S(2)}) %copy-start) | copy-done | bytes 1048600
  2.0 0.0 copy-start.1
  2.0 1.2 %copy-done.1 = bf16[1,128,4096]{2,1,0:T(8,128)(2,1)S(1)} copy-done((bf16[1,128,4096]{2,1,0:T(8,128)(2,1)S(1)}, bf16[1,128,4096]{2,1,0:T(8,128)(2,1)}, u32[]{:S(2)}) %copy-start.1) | copy-done | bytes 1048600
  3.2 0.0 copy-start.2
  3.2 1.2 %copy-done.2 = bf16[128,4096]{1,0:T(8,128)(2,1)S(1)} copy-done((bf16[128,4096]{1,0:T(8,128)(2,1)S(1)}, bf16[128,4096]{1,0:T(8,128)(2,1)}, u32[]{:S(2)}) %copy-start.2) | copy-done | bytes 1048600
  4.4 0.0 copy-start.3
  4.4 0.7 copy-done.3
  5.2 0.0 copy-start.4
  5.2 0.7 copy-done.4
  5.9 0.0 copy-start.5
  5.9 0.7 copy-done.5
  6.6 93.3 %shard_map.73 = bf16[1,128,4096]{2,1,0:T(8,128)(2,1)S(1)} custom-call(s32[16,4]{1,0:T(8,128)S(1)} %copy.8.list_ref, bf16[1,128,4096]{2,1,0:T(8,128)(2,1)S(1)} %copy-done, bf16[1,128,4096]{2,1,0:T(8,128)(2,1)S(1)} %copy-done.1, bf16[128,4096]{1,0:T(8,128)(2,1)S(1)} %copy-done.2, f32[1,4096]{1,0:T(1,128)S(1)} %copy-done.3, f32[1,4096]{1,0:T(1,128)S(1)} %copy-done.4, ...), custom_call_target="tpu_custom_call" | custom-call | tf_op jit(solution)/shard_map/pallas_call | solution.py:360
  99.9 1.0 copy.10
Async XLA Ops:
  0.8 1.2 %copy-start = (bf16[1,128,4096]{2,1,0:T(8,128)(2,1)S(1)}, bf16[1,128,4096]{2,1,0:T(8,128)(2,1)}, u32[]{:S(2)}) copy-start(bf16[1,128,4096]{2,1,0:T(8,128)(2,1)} %early_in.1) | copy-start | bytes 3145732
  2.0 1.2 %copy-start.1 = (bf16[1,128,4096]{2,1,0:T(8,128)(2,1)S(1)}, bf16[1,128,4096]{2,1,0:T(8,128)(2,1)}, u32[]{:S(2)}) copy-start(bf16[1,128,4096]{2,1,0:T(8,128)(2,1)} %cur_in.1) | copy-start | bytes 3145732
  3.2 1.2 %copy-start.2 = (bf16[128,4096]{1,0:T(8,128)(2,1)S(1)}, bf16[128,4096]{1,0:T(8,128)(2,1)}, u32[]{:S(2)}) copy-start(bf16[128,4096]{1,0:T(8,128)(2,1)} %next_in.1) | copy-start | bytes 3145732
  4.4 0.7 copy-start.3
  5.2 0.7 copy-start.4
  5.9 0.7 copy-start.5

commit v3 on v2

--- a/solution.py
+++ b/solution.py
@@ -14,6 +14,7 @@
 WIDTH = 4096
 CHUNKS = 16
 LAG = 2
+BEFORE = 3
 CHUNK = WIDTH // CHUNKS
 HALF = CHUNK // 2
 OUTER = 4
@@ -260,6 +261,7 @@
             swap_in(0, k, early_ref).start()
         swap_in(1, k, cur_ref).start()
 
+    def open_before(k):
         @pl.when(sends & is_last)
         def _():
             behind(0, k, early_ref).start()
@@ -296,6 +298,7 @@
             handoff(k).wait_recv()
         swap_in(2, k, second).start()
 
+    def open_second_before(k):
         @pl.when(is_last)
         def _():
             behind(1, k, cur_ref).start()
@@ -325,11 +328,13 @@
     def step(t):
         staged(0, t, lambda k: both(stage_select, k, early_ref, cur_ref))
         ychain.relay(t, 0, early_item)
+        staged(BEFORE, t, open_before)
         staged(first_y, t, lambda k: both(stage_y, k))
         zchain.relay(t, first_y, early_item)
         staged(first_z, t, lambda k: both(stage_z, k))
         staged(open_at, t, open_second)
         staged(pick_at, t, lambda k: stage_select(2, k, second))
+        staged(pick_at + BEFORE, t, open_second_before)
         ychain.relay(t, pick_at, late_item)
         staged(second_y, t, lambda k: stage_y(2, k))
         zchain.relay(t, second_y, late_item)

time: 101 us -> 97.6 us (0.966)
  Pallas kernels: 93.3 us -> 89.6 us
    pallas_call x1, Pallas kernels: 93.3 us -> 89.6 us  [local(): pl.pallas_call(functools.partial(kernel, n, sections), out_shape=jax.Shap...]
where the time goes in v3:
time: 97.6 us; the launch traced here: 97.1 us
  Pallas kernels  89.6 us (92%)
  local copies, waits for them, and re-layouts  7.55 us (8%)
    pallas_call x1, Pallas kernels, local(): pl.pallas_call(functools.partial(kernel, n, sections), out_shape=jax.Shap...  89.6 us
    unnamed x14, local copies, waits for them, and re-layouts  7.55 us

profile of v3, /device:TPU:0, one launch (start us, length us, event | category | flops | bytes accessed | tf_op | source)
XLA Modules:
  0.0 97.1 jit_solution(9196385862703320913)
XLA Ops:
  0.0 0.8 copy.8.list_ref
  0.8 0.0 copy-start
  0.8 1.2 %copy-done = bf16[1,128,4096]{2,1,0:T(8,128)(2,1)S(1)} copy-done((bf16[1,128,4096]{2,1,0:T(8,128)(2,1)S(1)}, bf16[1,128,4096]{2,1,0:T(8,128)(2,1)}, u32[]{:S(2)}) %copy-start) | copy-done | bytes 1048600
  2.0 0.0 copy-start.1
  2.0 1.2 %copy-done.1 = bf16[1,128,4096]{2,1,0:T(8,128)(2,1)S(1)} copy-done((bf16[1,128,4096]{2,1,0:T(8,128)(2,1)S(1)}, bf16[1,128,4096]{2,1,0:T(8,128)(2,1)}, u32[]{:S(2)}) %copy-start.1) | copy-done | bytes 1048600
  3.2 0.0 copy-start.2
  3.2 1.2 %copy-done.2 = bf16[128,4096]{1,0:T(8,128)(2,1)S(1)} copy-done((bf16[128,4096]{1,0:T(8,128)(2,1)S(1)}, bf16[128,4096]{1,0:T(8,128)(2,1)}, u32[]{:S(2)}) %copy-start.2) | copy-done | bytes 1048600
  4.4 0.0 copy-start.3
  4.4 0.7 copy-done.3
  5.2 0.0 copy-start.4
  5.2 0.7 copy-done.4
  5.9 0.0 copy-start.5
  5.9 0.7 copy-done.5
  6.6 89.6 %shard_map.73 = bf16[1,128,4096]{2,1,0:T(8,128)(2,1)S(1)} custom-call(s32[16,4]{1,0:T(8,128)S(1)} %copy.8.list_ref, bf16[1,128,4096]{2,1,0:T(8,128)(2,1)S(1)} %copy-done, bf16[1,128,4096]{2,1,0:T(8,128)(2,1)S(1)} %copy-done.1, bf16[128,4096]{1,0:T(8,128)(2,1)S(1)} %copy-done.2, f32[1,4096]{1,0:T(1,128)S(1)} %copy-done.3, f32[1,4096]{1,0:T(1,128)S(1)} %copy-done.4, ...), custom_call_target="tpu_custom_call" | custom-call | tf_op jit(solution)/shard_map/pallas_call | solution.py:365
  96.1 1.0 %copy.10 = bf16[1,128,4096]{2,1,0:T(8,128)(2,1)} copy(bf16[1,128,4096]{2,1,0:T(8,128)(2,1)S(1)} %shard_map.73) | data formatting | bytes 2097152
Async XLA Ops:
  0.8 1.2 %copy-start = (bf16[1,128,4096]{2,1,0:T(8,128)(2,1)S(1)}, bf16[1,128,4096]{2,1,0:T(8,128)(2,1)}, u32[]{:S(2)}) copy-start(bf16[1,128,4096]{2,1,0:T(8,128)(2,1)} %early_in.1) | copy-start | bytes 3145732
  2.0 1.2 %copy-start.1 = (bf16[1,128,4096]{2,1,0:T(8,128)(2,1)S(1)}, bf16[1,128,4096]{2,1,0:T(8,128)(2,1)}, u32[]{:S(2)}) copy-start(bf16[1,128,4096]{2,1,0:T(8,128)(2,1)} %cur_in.1) | copy-start | bytes 3145732
  3.2 1.2 %copy-start.2 = (bf16[128,4096]{1,0:T(8,128)(2,1)S(1)}, bf16[128,4096]{1,0:T(8,128)(2,1)}, u32[]{:S(2)}) copy-start(bf16[128,4096]{1,0:T(8,128)(2,1)} %next_in.1) | copy-start | bytes 3145732
  4.4 0.7 copy-start.3
  5.2 0.7 copy-start.4
  5.9 0.7 copy-start.5

commit v4 on v3

--- a/solution.py
+++ b/solution.py
@@ -14,7 +14,7 @@
 WIDTH = 4096
 CHUNKS = 16
 LAG = 2
-BEFORE = 3
+BEFORE = 5
 CHUNK = WIDTH // CHUNKS
 HALF = CHUNK // 2
 OUTER = 4
@@ -318,12 +318,12 @@
     late_item = [(s >= 0, 2)]
     first_y = spread
     first_z = first_y + span
-    first_end = first_z + LAG
-    open_at = first_end + LAG
+    first_end = first_z + 1
+    open_at = first_end + 1
     pick_at = open_at + 1
     second_y = pick_at + spread
     second_z = second_y + span
-    second_end = second_z + LAG
+    second_end = second_z + 1
 
     def step(t):
         staged(0, t, lambda k: both(stage_select, k, early_ref, cur_ref))

time: 97.6 us -> 96.5 us (0.989); the launches traced: 97.1 us -> 94.7 us
  Pallas kernels: 89.6 us -> 87.2 us
    pallas_call x1, Pallas kernels: 89.6 us -> 87.2 us  [local(): pl.pallas_call(functools.partial(kernel, n, sections), out_shape=jax.Shap...]
where the time goes in v4:
time: 96.5 us; the launch traced here: 94.7 us
  Pallas kernels  87.2 us (90%)
  local copies, waits for them, and re-layouts  7.55 us (8%)
    pallas_call x1, Pallas kernels, local(): pl.pallas_call(functools.partial(kernel, n, sections), out_shape=jax.Shap...  87.2 us
    unnamed x14, local copies, waits for them, and re-layouts  7.55 us

profile of v4, /device:TPU:0, one launch (start us, length us, event | category | flops | bytes accessed | tf_op | source)
XLA Modules:
  0.0 94.7 jit_solution(7062706968991638200)
XLA Ops:
  0.0 0.8 copy.8.list_ref
  0.8 0.0 copy-start
  0.8 1.2 %copy-done = bf16[1,128,4096]{2,1,0:T(8,128)(2,1)S(1)} copy-done((bf16[1,128,4096]{2,1,0:T(8,128)(2,1)S(1)}, bf16[1,128,4096]{2,1,0:T(8,128)(2,1)}, u32[]{:S(2)}) %copy-start) | copy-done | bytes 1048600
  2.0 0.0 copy-start.1
  2.0 1.2 %copy-done.1 = bf16[1,128,4096]{2,1,0:T(8,128)(2,1)S(1)} copy-done((bf16[1,128,4096]{2,1,0:T(8,128)(2,1)S(1)}, bf16[1,128,4096]{2,1,0:T(8,128)(2,1)}, u32[]{:S(2)}) %copy-start.1) | copy-done | bytes 1048600
  3.2 0.0 copy-start.2
  3.2 1.2 %copy-done.2 = bf16[128,4096]{1,0:T(8,128)(2,1)S(1)} copy-done((bf16[128,4096]{1,0:T(8,128)(2,1)S(1)}, bf16[128,4096]{1,0:T(8,128)(2,1)}, u32[]{:S(2)}) %copy-start.2) | copy-done | bytes 1048600
  4.4 0.0 copy-start.3
  4.4 0.7 copy-done.3
  5.2 0.0 copy-start.4
  5.2 0.7 copy-done.4
  5.9 0.0 copy-start.5
  5.9 0.7 copy-done.5
  6.6 87.2 %shard_map.73 = bf16[1,128,4096]{2,1,0:T(8,128)(2,1)S(1)} custom-call(s32[16,4]{1,0:T(8,128)S(1)} %copy.8.list_ref, bf16[1,128,4096]{2,1,0:T(8,128)(2,1)S(1)} %copy-done, bf16[1,128,4096]{2,1,0:T(8,128)(2,1)S(1)} %copy-done.1, bf16[128,4096]{1,0:T(8,128)(2,1)S(1)} %copy-done.2, f32[1,4096]{1,0:T(1,128)S(1)} %copy-done.3, f32[1,4096]{1,0:T(1,128)S(1)} %copy-done.4, ...), custom_call_target="tpu_custom_call" | custom-call | tf_op jit(solution)/shard_map/pallas_call | solution.py:365
  93.7 1.0 %copy.10 = bf16[1,128,4096]{2,1,0:T(8,128)(2,1)} copy(bf16[1,128,4096]{2,1,0:T(8,128)(2,1)S(1)} %shard_map.73) | data formatting | bytes 2097152
Async XLA Ops:
  0.8 1.2 %copy-start = (bf16[1,128,4096]{2,1,0:T(8,128)(2,1)S(1)}, bf16[1,128,4096]{2,1,0:T(8,128)(2,1)}, u32[]{:S(2)}) copy-start(bf16[1,128,4096]{2,1,0:T(8,128)(2,1)} %early_in.1) | copy-start | bytes 3145732
  2.0 1.2 %copy-start.1 = (bf16[1,128,4096]{2,1,0:T(8,128)(2,1)S(1)}, bf16[1,128,4096]{2,1,0:T(8,128)(2,1)}, u32[]{:S(2)}) copy-start(bf16[1,128,4096]{2,1,0:T(8,128)(2,1)} %cur_in.1) | copy-start | bytes 3145732
  3.2 1.2 %copy-start.2 = (bf16[128,4096]{1,0:T(8,128)(2,1)S(1)}, bf16[128,4096]{1,0:T(8,128)(2,1)}, u32[]{:S(2)}) copy-start(bf16[128,4096]{1,0:T(8,128)(2,1)} %next_in.1) | copy-start | bytes 3145732
  4.4 0.7 copy-start.3
  5.2 0.7 copy-start.4
  5.9 0.7 copy-start.5
